TPU v7x, 32 devices: a whole 2x2x4 slice. The times are simulated.
32 devices in a mesh: ctx: 4 (over y, x), exp: 4 (over z), dp: 2 (over core).
Axes of the slice: x: 2, y: 2, z: 4, core: 2. Of those that a mesh axis runs over, the one named last changes fastest.
Arguments:
- queries: bfloat16 [8, 768, 2048], P(('dp', 'exp'), 'ctx'), parts along dimension 0, may hold values from -38 to 38
- keys: bfloat16 [8, 768, 256], P(('dp', 'exp'), 'ctx'), parts along dimension 0, may hold values from -4 to 4
- values: bfloat16 [8, 768, 256], P(('dp', 'exp'), 'ctx'), parts along dimension 0, may hold values from -6 to 6
- segments: int32 [8, 768], P(('dp', 'exp')), parts along dimension 0, may hold values from 0 to 7, never falling along the last dimension, each value on 1 to 384 neighbouring positions
- residual: bfloat16 [8, 768, 1024], P(('dp', 'exp'), 'ctx'), parts along dimension 0, may hold values from -3 to 3
- out_weight: bfloat16 [2048, 1024], P('ctx'), may hold values from -0.125 to 0.125
- gain: float32 [1024], replicated, may hold values from 0.1 to 1.9
- expert_ids: int32 [8, 768, 8], P(('dp', 'exp'), 'ctx'), parts along dimension 0, may hold values from 0 to 127, all different within a row; in each aligned block of 192 rows (0 to 191, 192 to 383, ..., all dimensions but the last counted through in order) at most 24 rows name the same one
- route_weights: float32 [8, 768, 8], P(('dp', 'exp'), 'ctx'), parts along dimension 0, may hold values from 0.05 to 0.5
- w_gate: bfloat16 [4, 1024, 384], P('exp'), may hold values from -0.1875 to 0.1875
- w_up: bfloat16 [4, 1024, 384], P('exp'), may hold values from -0.1875 to 0.1875
- w_down: bfloat16 [4, 384, 1024], P('exp'), may hold values from -0.3125 to 0.3125
Outputs:
- layer_out: bfloat16 [8, 768, 1024], P(('dp', 'exp'), 'ctx'), parts along dimension 0
There are 2 independent parts, one for each index of `dp`. A program takes and returns all parts, laid end to end along the dimension named above; an argument that names none is the same for every part. Nothing has to cross between parts.
Inputs may be any that keep to these rules, and one draw needn't show every extreme that they name: `expert_ids`: in every aligned block of 192 positions of a sequence (one slab), no expert is named by more than 24 tokens, and in every draw some expert is named by exactly 24 tokens of some block; a token names 8 different experts. `segments`: document numbers never fall along a sequence.
All inputs are finite; a program needn't handle non-finite values.
Results may differ from a plain program's by a relative error of at most 0.006.
Values may be sent and summed in bfloat16 or wider, within the bound.
No kernel may reach another device: no remote copies, remote signals or barrier semaphores. Data moves between devices by JAX's collectives and lax.ppermute only.
A program may use at most 64 MiB of HBM per device.

v0:
```python
import functools
import math

import jax
import jax.numpy as jnp
from jax import lax
from jax.experimental import pallas as pl
from jax.experimental.pallas import tpu as pltpu
from jax.sharding import PartitionSpec as P

HQ = 16
KVH = 2
HD = 128
GROUPS = HQ // KVH
CAP = 24
NEG = -1e30
SCORE_SCALE = math.log2(math.e) / math.sqrt(HD)
F32 = jnp.float32
BF16 = jnp.bfloat16


def slab_segments(segs_ref, index, count, rows):
    found = segs_ref[:, 0:rows]
    for slab in range(1, count):
        found = jnp.where(index == slab, segs_ref[:, slab * rows : (slab + 1) * rows], found)
    return found


def score_bias(segs_ref, backs, count, rows):
    me = lax.axis_index("ctx")
    row = lax.broadcasted_iota(jnp.int32, (rows, rows), 0)
    col = lax.broadcasted_iota(jnp.int32, (rows, rows), 1)
    own_seg = slab_segments(segs_ref, me, count, rows)
    query_seg = jnp.sum(jnp.where(row == col, own_seg, 0), axis=1, keepdims=True)
    parts = []
    for back in backs:
        if back == 0:
            allowed = (col <= row) & (own_seg == query_seg)
        else:
            key_seg = slab_segments(segs_ref, jnp.maximum(me - back, 0), count, rows)
            allowed = (key_seg == query_seg) & (me >= back)
        parts.append(jnp.where(allowed, 0.0, NEG))
    return parts


def group_scores(stacked, keys, bias):
    scores = lax.dot_general(
        stacked, keys, (((1,), (1,)), ((), ())), preferred_element_type=F32
    )
    return scores.reshape(GROUPS, *bias.shape) * SCORE_SCALE + bias


def weigh(expo, values):
    rows = expo.shape[0] * expo.shape[1]
    mixed = jnp.dot(
        expo.astype(BF16).reshape(rows, expo.shape[2]), values, preferred_element_type=F32
    ).reshape(*expo.shape[:2], 2 * HD)
    return mixed[:, :, :HD], mixed[:, :, HD:]


def mark_kernel(*refs):
    refs[-1][...] = jnp.zeros_like(refs[-1])


def gate_kernel(*refs):
    del refs


def after(piece, *marks):
    spec = pl.BlockSpec(memory_space=pl.ANY)
    return pl.pallas_call(
        gate_kernel,
        out_shape=jax.ShapeDtypeStruct(piece.shape, piece.dtype),
        in_specs=[spec] * (1 + len(marks)),
        out_specs=spec,
        input_output_aliases={0: 0},
        compiler_params=pltpu.CompilerParams(vmem_limit_bytes=1 << 20),
    )(piece, *marks)


def join_kernel(first_ref, second_ref, mark_ref, whole_ref, sems):
    del mark_ref
    half = first_ref.shape[0]
    core = lax.rem(lax.axis_index("dp"), 2)
    copies = []
    for index, (lead, ref) in enumerate([(core, first_ref), (1 - core, second_ref)]):
        target = whole_ref.at[pl.ds(pl.multiple_of(lead * half, half), half)]
        copies.append(pltpu.make_async_copy(ref, target, sems.at[index]))
        copies[-1].start()
    for copy in copies:
        copy.wait()


def own_kernel(
    n_ctx,
    q_ref,
    kv_ref,
    segs_ref,
    mark_ref,
    w_ref,
    acc_ref,
    max_ref,
    sum_ref,
    queries_ref,
    first_ref,
    second_ref,
    sems,
):
    del mark_ref
    half = first_ref.shape[0]
    core = lax.rem(lax.axis_index("dp"), 2)
    copies = []
    for index, (lead, ref) in enumerate([(core, first_ref), (1 - core, second_ref)]):
        source = w_ref.at[pl.ds(pl.multiple_of(lead * half, half), half)]
        copies.append(pltpu.make_async_copy(source, ref, sems.at[index]))
        copies[-1].start()
    rows = q_ref.shape[0]
    (bias,) = score_bias(segs_ref, (0,), n_ctx, rows)
    ones = jnp.ones((rows, HD), BF16)
    for kv in range(KVH):
        keys = kv_ref[:, kv * HD : (kv + 1) * HD]
        values = jnp.concatenate([kv_ref[:, (KVH + kv) * HD : (KVH + kv + 1) * HD], ones], axis=1)
        heads = range(kv * GROUPS, (kv + 1) * GROUPS)
        stacked = jnp.concatenate([q_ref[:, h * HD : (h + 1) * HD] for h in heads], axis=0)
        queries_ref[kv] = stacked
        scores = group_scores(stacked, keys, bias)
        row_max = jnp.max(scores, axis=2, keepdims=True)
        accum, row_sum = weigh(jnp.exp2(scores - row_max), values)
        acc_ref[kv] = accum
        max_ref[kv] = jnp.broadcast_to(row_max, max_ref.shape[1:])
        sum_ref[kv] = row_sum
    for copy in copies:
        copy.wait()


def route_kernel(ids_ref, rw_ref, res_ref, place_ref, mix_ref, rows_ref):
    slots, rows = place_ref.shape
    slot = lax.broadcasted_iota(jnp.int32, (slots, rows), 0)
    owner = (slot // CAP) ^ lax.axis_index("exp")
    hit = jnp.zeros((slots, rows), jnp.bool_)
    weight = jnp.zeros((slots, rows), F32)
    for choice in range(ids_ref.shape[0]):
        same = ids_ref[choice : choice + 1, :] == owner
        hit = hit | same
        weight = jnp.where(same, rw_ref[choice : choice + 1, :], weight)
    row = lax.broadcasted_iota(jnp.int32, (rows, rows), 0)
    col = lax.broadcasted_iota(jnp.int32, (rows, rows), 1)
    before = (row < col).astype(F32).astype(BF16)
    rank = jnp.dot(hit.astype(F32).astype(BF16), before, preferred_element_type=F32)
    placed = hit & (rank == lax.rem(slot, CAP).astype(F32))
    place = placed.astype(F32).astype(BF16)
    place_ref[...] = place
    mix = jnp.where(placed, weight, 0.0)
    high = mix.astype(BF16).astype(F32)
    mix_ref[...] = jnp.concatenate([high, mix - high], axis=0).T.astype(BF16)
    rows_ref[...] = jnp.dot(place, res_ref[...], preferred_element_type=F32)


def rest_kernel(
    n_ctx,
    back_count,
    segs_ref,
    acc_ref,
    max_ref,
    sum_ref,
    queries_ref,
    place_ref,
    *refs,
):
    kv_refs, (out_ref, routed_ref) = refs[:back_count], refs[-2:]
    rows = queries_ref.shape[1] // GROUPS
    bias = jnp.concatenate(score_bias(segs_ref, range(1, back_count + 1), n_ctx, rows), axis=1)
    keys_count = rows * back_count
    spread = -(-keys_count // HD)
    ones = jnp.ones((keys_count, HD), BF16)
    scores = []
    for kv in range(KVH):
        keys = jnp.concatenate([ref[:, kv * HD : (kv + 1) * HD] for ref in kv_refs], axis=0)
        scores.append(group_scores(queries_ref[kv], keys, bias))
    for kv in range(KVH):
        values = jnp.concatenate(
            [ref[:, (KVH + kv) * HD : (KVH + kv + 1) * HD] for ref in kv_refs], axis=0
        )
        values = jnp.concatenate([values, ones], axis=1)
        old_max = max_ref[kv]
        new_max = jnp.maximum(old_max, jnp.max(scores[kv], axis=2, keepdims=True))
        shift = jnp.concatenate([new_max] * spread, axis=2)[:, :, :keys_count]
        accum, row_sum = weigh(jnp.exp2(scores[kv] - shift), values)
        fix = jnp.exp2(old_max - new_max)
        total = sum_ref[kv] * fix + row_sum
        attended = ((acc_ref[kv] * fix + accum) / total).astype(BF16)
        for group in range(GROUPS):
            head = kv * GROUPS + group
            out_ref[:, head * HD : (head + 1) * HD] = attended[group]
    routed_ref[...] = jnp.dot(place_ref[...], out_ref[...], preferred_element_type=F32)


def send_kernel(blocks, entries, owners, routed_ref, rows_ref, *refs):
    piece_refs, send_refs = refs[:-owners], refs[-owners:]
    me, core = lax.axis_index("ctx"), lax.axis_index("dp")
    share = routed_ref.shape[1] // lax.axis_size("ctx")
    part = project(rows_ref[...], routed_ref, entries, piece_refs, False)
    for step, ref in enumerate(send_refs):
        rows = pl.ds(step * CAP, CAP)
        filled = 0
        for size, flip, offset in blocks:
            lead = pl.multiple_of((me ^ flip(core)) * share + offset(core), size)
            ref[:, filled : filled + size] = routed_ref[rows, pl.ds(lead, size)].astype(BF16)
            filled += size
        ref[:, filled:] = part[step * CAP : (step + 1) * CAP, :].astype(BF16)


def stack(parts):
    return jnp.concatenate([part.astype(F32) for part in parts], axis=0).astype(BF16)


def project(total, att_ref, entries, piece_refs, moved):
    me, core = lax.axis_index("ctx"), lax.axis_index("dp")
    share = att_ref.shape[1] // lax.axis_size("ctx")
    for piece, size, flip, offset, row, column in entries:
        lead = column(core) if moved else (me ^ flip(core)) * share + offset(core)
        columns = pl.ds(pl.multiple_of(lead, size), size)
        rows = pl.ds(pl.multiple_of(row(me, core), size), size)
        total = total + jnp.dot(
            att_ref[:, columns].astype(BF16),
            piece_refs[piece][rows, :],
            preferred_element_type=F32,
        )
    return total


def arrive_kernel(owners, entries, *refs):
    row_refs, piece_refs, (att_ref, hidden_ref) = refs[:owners], refs[owners:-2], refs[-2:]
    row_refs = row_refs[:1] + row_refs[:0:-1]
    wide = att_ref.shape[1]
    att_ref[...] = stack([ref[:, :wide] for ref in row_refs])
    hidden = jnp.concatenate([ref[:, wide:].astype(F32) for ref in row_refs], axis=0)
    hidden_ref[...] = project(hidden, att_ref, entries, piece_refs, True)


def expert_kernel(entries, count, gain_ref, gate_ref, up_ref, down_ref, att_ref, part_ref, *refs):
    piece_refs, out_refs = refs[:count], refs[count:]
    hidden = project(part_ref[...], att_ref, entries, piece_refs, True)
    mean = jnp.mean(hidden * hidden, axis=1, keepdims=True)
    normed = (hidden * lax.rsqrt(mean + 1e-06) * gain_ref[...]).astype(BF16)
    gate = jnp.dot(normed, gate_ref[...], preferred_element_type=F32)
    up = jnp.dot(normed, up_ref[...], preferred_element_type=F32)
    act = (gate / (1.0 + jnp.exp(-gate)) * up).astype(BF16)
    out = jnp.dot(act, down_ref[...], preferred_element_type=F32)
    for step, ref in enumerate(out_refs):
        ref[...] = out[step * CAP : (step + 1) * CAP, :].astype(BF16)


def project_kernel(entries, att_ref, res_ref, *refs):
    hidden = res_ref[...].astype(F32)
    refs[-1][...] = project(hidden, att_ref, entries, refs[:-1], False)


def combine_kernel(owners, hidden_ref, mix_ref, *refs):
    row_refs, out_ref = refs[:1] + refs[owners - 1 : 0 : -1], refs[owners]
    rows = stack([ref[...] for ref in row_refs])
    total = hidden_ref[...] + jnp.dot(
        mix_ref[...], jnp.concatenate([rows, rows], axis=0), preferred_element_type=F32
    )
    out_ref[...] = total.astype(BF16)


def call(kernel, outs, args, micros, scratch=(), limit=24, free_in=0, free_out=0):
    vmem, free = pl.BlockSpec(memory_space=pltpu.VMEM), pl.BlockSpec(memory_space=pl.ANY)
    nbytes = sum(math.prod(a.shape) * a.dtype.itemsize for a in list(args) + list(outs))
    return pl.pallas_call(
        kernel,
        out_shape=outs,
        in_specs=[vmem] * (len(args) - free_in) + [free] * free_in,
        out_specs=[vmem] * (len(outs) - free_out) + [free] * free_out,
        scratch_shapes=list(scratch),
        compiler_params=pltpu.CompilerParams(vmem_limit_bytes=limit << 20),
        cost_estimate=pl.CostEstimate(
            flops=int(micros * 1.15e9), bytes_accessed=nbytes, transcendentals=0
        ),
    )(*args)


def exchange(blocks):
    count = len(blocks)
    return [blocks[0]] + [
        lax.ppermute(blocks[s], "exp", [(i, i ^ s) for i in range(count)])
        for s in range(count - 1, 0, -1)
    ]


def gather_weight(weight, first, second, attended):
    n_ctx, cores = lax.axis_size("ctx"), lax.axis_size("dp")
    share = weight.shape[0]
    if (n_ctx, cores) != (4, 2):
        whole = lax.all_gather(weight, "ctx", axis=0, tiled=True)
        entries = [
            (
                0,
                share,
                lambda core, f=f: f,
                lambda core: 0,
                lambda me, core, f=f: (me ^ f) * share,
                lambda core, f=f: (f - 1) * share,
            )
            for f in range(n_ctx)
        ]
        home = [(0, share, lambda core: 0, lambda core: 0, lambda me, core: 0, None)]
        blocks = [(share, lambda core, f=f: f, lambda core: 0) for f in range(1, n_ctx)]
        return [whole], entries, entries[1:], [weight], home, blocks
    both = ("ctx", "dp")
    devices = [(me, core) for me in range(n_ctx) for core in range(cores)]
    aside = [(me * 2 + core, (me ^ (1 + core)) * 2 + core) for me, core in devices]
    across = [(me * 2 + core, (me ^ (2 - core)) * 2 + core) for me, core in devices]
    near_first = lax.ppermute(first, both, aside)
    near_second = lax.ppermute(second, both, aside)
    near_first = after(near_first, attended)
    far = lax.ppermute(near_first, both, across)
    (near,) = call(
        join_kernel,
        [jax.ShapeDtypeStruct(weight.shape, BF16)],
        [near_first, near_second, attended],
        micros=1,
        free_in=3,
        free_out=1,
        limit=1,
        scratch=[pltpu.SemaphoreType.DMA((2,))],
    )
    swap = [(0, 1), (1, 0)]
    pieces = [weight, near, far, lax.ppermute(near, "dp", swap), lax.ppermute(far, "dp", swap)]
    half = share // 2
    top = lambda me, core: 0
    entries = [
        (0, share, lambda core: 0, lambda core: 0, top, None),
        (1, share, lambda core: 1 + core, lambda core: 0, top, None),
        (2, half, lambda core: 3, lambda core: core * half, top, None),
        (3, share, lambda core: 2 - core, lambda core: 0, top, None),
        (4, half, lambda core: 3, lambda core: (1 - core) * half, top, None),
    ]
    moved = [
        (1, half, None, None, lambda me, core: (1 - core) * half, lambda core: 0),
        (2, half, None, None, top, lambda core: (3 + core) * half),
        (3, half, None, None, top, lambda core: half),
        (3, half, None, None, lambda me, core: half, lambda core: 2 * half),
        (4, half, None, None, top, lambda core: (4 - core) * half),
    ]
    home = [
        (0, share, lambda core: 0, lambda core: 0, top, None),
        (1, half, lambda core: 1 + core, lambda core: core * half, top, None),
    ]
    blocks = [
        (half, lambda core: 1 + core, lambda core: (1 - core) * half),
        (share, lambda core: 2 - core, lambda core: 0),
        (share, lambda core: 3, lambda core: 0),
    ]
    return pieces, entries, moved, [weight, near_first], home, blocks


def per_device(
    queries,
    keys,
    values,
    segments,
    residual,
    out_weight,
    gain,
    expert_ids,
    route_weights,
    w_gate,
    w_up,
    w_down,
):
    tok_rows = queries.shape[1]
    width = residual.shape[2]
    att_width = queries.shape[2]
    n_ctx, owners = lax.axis_size("ctx"), lax.axis_size("exp")
    slots = owners * CAP
    longest = segments.shape[1] // 2
    back_count = min(n_ctx - 1, -(-(longest - 1) // tok_rows))
    shape = jax.ShapeDtypeStruct

    own_kv = jnp.concatenate([keys[0], values[0]], axis=1)
    kv_blocks = []
    for back in range(1, back_count + 1):
        pairs = [(i, (i + back) % n_ctx) for i in range(n_ctx)]
        kv_blocks.append(lax.ppermute(own_kv, "ctx", pairs))
    (mark,) = call(mark_kernel, [shape((8, 128), F32)], [own_kv], micros=5, free_in=1, limit=1)
    half = shape((out_weight.shape[0] // 2, width), BF16)
    accum, row_max, row_sum, stacked, first, second = call(
        functools.partial(own_kernel, n_ctx),
        [
            shape((KVH, GROUPS, tok_rows, HD), F32),
            shape((KVH, GROUPS, tok_rows, HD), F32),
            shape((KVH, GROUPS, tok_rows, HD), F32),
            shape((KVH, GROUPS * tok_rows, HD), BF16),
            half,
            half,
        ],
        [queries[0], own_kv, segments, mark, out_weight],
        micros=3,
        free_in=1,
        free_out=2,
        scratch=[pltpu.SemaphoreType.DMA((2,))],
    )
    place, mix, res_rows = call(
        route_kernel,
        [
            shape((slots, tok_rows), BF16),
            shape((tok_rows, 2 * slots), BF16),
            shape((slots, width), F32),
        ],
        [expert_ids[0].T, route_weights[0].T, residual[0]],
        micros=1,
    )
    attended, chosen = call(
        functools.partial(rest_kernel, n_ctx, back_count),
        [shape((tok_rows, att_width), BF16), shape((slots, att_width), F32)],
        [segments, accum, row_max, row_sum, stacked, place, *kv_blocks]
        + [gain[None, :], w_gate[0], w_up[0], w_down[0]],
        micros=5,
    )
    pieces, entries, moved, near, home, blocks = gather_weight(
        out_weight, first, second, attended
    )
    moved_width = sum(size for size, _, _ in blocks)
    routed = call(
        functools.partial(send_kernel, blocks, home, owners),
        [shape((CAP, moved_width + width), BF16)] * owners,
        [chosen, res_rows, *near],
        micros=1,
    )
    early = pieces[1:2]
    late = pieces[2:] or pieces
    now = [(0, *entry[1:]) for entry in moved if early and entry[0] == 1]
    skipped = len(pieces) - len(late)
    then = [(entry[0] - skipped, *entry[1:]) for entry in moved if entry[0] >= skipped]
    arrived, part = call(
        functools.partial(arrive_kernel, owners, now),
        [shape((slots, moved_width), BF16), shape((slots, width), F32)],
        [*exchange(routed), *early],
        micros=10,
    )
    done = call(
        functools.partial(expert_kernel, then, len(late)),
        [shape((CAP, width), BF16)] * owners,
        [gain[None, :], w_gate[0], w_up[0], w_down[0], arrived, part, *late],
        micros=2,
    )
    back = exchange(done)
    (hidden,) = call(
        functools.partial(project_kernel, entries),
        [shape((tok_rows, width), F32)],
        [attended, residual[0], *pieces],
        micros=2,
    )
    (out,) = call(
        functools.partial(combine_kernel, owners),
        [shape((tok_rows, width), BF16)],
        [hidden, mix, *back],
        micros=1,
    )
    return out[None]


def solution(mesh):
    return jax.shard_map(
        per_device,
        mesh=mesh,
        in_specs=(
            P(("dp", "exp"), "ctx", None),
            P(("dp", "exp"), "ctx", None),
            P(("dp", "exp"), "ctx", None),
            P(("dp", "exp"), None),
            P(("dp", "exp"), "ctx", None),
            P("ctx", None),
            P(),
            P(("dp", "exp"), "ctx", None),
            P(("dp", "exp"), "ctx", None),
            P("exp", None, None),
            P("exp", None, None),
            P("exp", None, None),
        ),
        out_specs=P(("dp", "exp"), "ctx", None),
        check_vma=False,
    )
```

profile of v0, /device:TPU:0, one launch (start us, length us, event | category | flops | bytes accessed | tf_op | source)
XLA Modules:
  0.0 43.1 jit_solution(10449269820288744550)
XLA Ops:
  0.0 1.0 %pad_maximum_fusion.refs_0_.kv_ref = bf16[192,512]{1,0:T(8,128)(2,1)S(1)} fusion(bf16[192,256]{1,0:T(8,128)(2,1)} %bitcast.28, bf16[192,256]{1,0:T(8,128)(2,1)} %bitcast.29), kind=kLoop, calls=%fused_computation | loop fusion | flops 393216 | bytes 393216 | tf_op jit(solution)/shard_map/concatenate | solution.py:382
  1.0 3.0 %collective-permute-start.1 = (bf16[192,512]{1,0:T(8,128)(2,1)S(1)}, bf16[192,512]{1,0:T(8,128)(2,1)S(1)}, u32[]{:S(2)}, u32[]{:S(2)}) collective-permute-start(bf16[192,512]{1,0:T(8,128)(2,1)S(1)} %pad_maximum_fusion.refs_0_.kv_ref), channel_id=1, source_target_pairs={{0,16},{8,24},{16,0},{24,8},{1,17},{9,25},{17,1},{25,9},{2,18},{10... | collective-permute-start | bytes 589832 | tf_op jit(solution)/shard_map/ppermute | solution.py:386
  4.0 1.5 %collective-permute-start = (bf16[192,512]{1,0:T(8,128)(2,1)S(1)}, bf16[192,512]{1,0:T(8,128)(2,1)S(1)}, u32[]{:S(2)}, u32[]{:S(2)}) collective-permute-start(bf16[192,512]{1,0:T(8,128)(2,1)S(1)} %pad_maximum_fusion.refs_0_.kv_ref), channel_id=1, source_target_pairs={{0,8},{8,16},{16,24},{24,0},{1,9},{9,17},{17,25},{25,1},{2,10},{10... | collective-permute-start | bytes 589832 | tf_op jit(solution)/shard_map/ppermute | solution.py:386
  5.6 1.9 %shard_map.119 = (f32[2,8,192,128]{3,2,1,0:T(8,128)S(1)}, f32[2,8,192,128]{3,2,1,0:T(8,128)S(1)}, f32[2,8,192,128]{3,2,1,0:T(8,128)S(1)}, bf16[2,1536,128]{2,1,0...) custom-call(bf16[192,2048]{1,0:T(8,128)(2,1)S(1)} %bitcast.15, ...), custom_call_target="tpu_custom_call" | custom-call | flops 3449999872 | bytes 8592384 | tf_op jit(solution)/shard_map/pallas_call | solution.py:271
  7.4 0.1 collective-permute-start.2
  7.5 2.0 %collective-permute-start.3 = (bf16[256,1024]{1,0:T(8,128)(2,1)S(1)}, bf16[256,1024]{1,0:T(8,128)(2,1)S(1)}, u32[]{:S(2)}, u32[]{:S(2)}) collective-permute-start(bf16[256,1024]{1,0:T(8,128)(2,1)S(1)} %get-tuple-element.33), channel_id=1, source_target_pairs={{0,8},{1,17},{8,0},{9,25},{16,24},{17,1},{24,16},{25,9},{2,10},{3,... | collective-permute-start | bytes 1572872 | tf_op jit(solution)/shard_map/ppermute | solution.py:316
  9.6 0.4 shard_map.120
  10.0 4.0 %collective-permute-done.1.refs_1_ = bf16[192,512]{1,0:T(8,128)(2,1)S(1)} collective-permute-done((bf16[192,512]{1,0:T(8,128)(2,1)S(1)}, bf16[192,512]{1,0:T(8,128)(2,1)S(1)}, u32[]{:S(2)}, u32[]{:S(2)}) %collective-permute-start.1) | collective-permute-done | bytes 196640 | tf_op jit(solution)/shard_map/ppermute | solution.py:386
  14.0 2.8 %shard_map.121 = (bf16[192,2048]{1,0:T(8,128)(2,1)S(1)}, f32[96,2048]{1,0:T(8,128)S(1)}) custom-call(s32[1,768]{1,0:T(1,128)S(1)} %copy-done.9, f32[2,8,192,128]{3,2,1,0:T(8,128)S(1)} %get-tuple-element.26.acc_ref, f32[2,8,192,128]{3,2,1,0:T(8,128)S(1)} %get-tuple-element.27.max_ref, f32[2,8,192,128]{3,2,1,0:T(8,128)S(1)} %get-tuple-element.28.sum_ref, ...), custom_call_target="tpu_custom_call" | custom-call | flops 5750000128 | bytes 9874432 | tf_op jit(solution)/shard_map/pallas_call | solution.py:271
  16.8 2.0 %collective-permute-start.4 = (bf16[256,1024]{1,0:T(8,128)(2,1)S(1)}, bf16[256,1024]{1,0:T(8,128)(2,1)S(1)}, u32[]{:S(2)}, u32[]{:S(2)}) collective-permute-start(bf16[256,1024]{1,0:T(8,128)(2,1)S(1)} %shard_map.122.first_ref.refs_1_), channel_id=1, source_target_pairs={{0,16},{1,9},{8,24},{9,1},{16,0},{17,25},{24,8},{25,17},{2,18},{3,... | collective-permute-start | bytes 1572872 | tf_op jit(solution)/shard_map/ppermute | solution.py:318
  18.9 0.4 shard_map.125
  19.3 3.7 %collective-permute-start.7 = (bf16[24,2304]{1,0:T(8,128)(2,1)S(1)}, bf16[24,2304]{1,0:T(8,128)(2,1)S(1)}, u32[]{:S(2)}, u32[]{:S(2)}) collective-permute-start(bf16[24,2304]{1,0:T(8,128)(2,1)S(1)} %get-tuple-element.38), channel_id=1, source_target_pairs={{0,6},{2,4},{4,2},{6,0},{1,7},{3,5},{5,3},{7,1},{8,14},{10,12},{12... | collective-permute-start | bytes 331784 | tf_op jit(solution)/shard_map/ppermute | solution.py:287
  23.0 0.7 %collective-permute-start.9 = (bf16[24,2304]{1,0:T(8,128)(2,1)S(1)}, bf16[24,2304]{1,0:T(8,128)(2,1)S(1)}, u32[]{:S(2)}, u32[]{:S(2)}) collective-permute-start(bf16[24,2304]{1,0:T(8,128)(2,1)S(1)} %get-tuple-element.40), channel_id=1, source_target_pairs={{0,2},{2,0},{4,6},{6,4},{1,3},{3,1},{5,7},{7,5},{8,10},{10,8},{12,... | collective-permute-start | bytes 331784 | tf_op jit(solution)/shard_map/ppermute | solution.py:287
  23.8 4.7 %collective-permute-start.5 = (bf16[512,1024]{1,0:T(8,128)(2,1)S(1)}, bf16[512,1024]{1,0:T(8,128)(2,1)S(1)}, u32[]{:S(2)}, u32[]{:S(2)}) collective-permute-start(bf16[512,1024]{1,0:T(8,128)(2,1)S(1)} %shard_map.123.refs_1_.refs_4_), channel_id=1, source_target_pairs={{0,1},{1,0},{2,3},{3,2},{4,5},{5,4},{6,7},{7,6},{8,9},{9,8},{10,11... | collective-permute-start | bytes 3145736 | tf_op jit(solution)/shard_map/ppermute | solution.py:330
  28.5 1.5 %collective-permute-done.4.refs_2_.refs_0_ = bf16[256,1024]{1,0:T(8,128)(2,1)S(1)} collective-permute-done((bf16[256,1024]{1,0:T(8,128)(2,1)S(1)}, bf16[256,1024]{1,0:T(8,128)(2,1)S(1)}, u32[]{:S(2)}, u32[]{:S(2)}) %collective-permute-start.4) | collective-permute-done | bytes 524320 | tf_op jit(solution)/shard_map/ppermute | solution.py:318
  30.0 2.6 %collective-permute-done.8.refs_2_ = bf16[24,2304]{1,0:T(8,128)(2,1)S(1)} collective-permute-done((bf16[24,2304]{1,0:T(8,128)(2,1)S(1)}, bf16[24,2304]{1,0:T(8,128)(2,1)S(1)}, u32[]{:S(2)}, u32[]{:S(2)}) %collective-permute-start.8) | collective-permute-done | bytes 110624 | tf_op jit(solution)/shard_map/ppermute | solution.py:287
  32.6 0.2 shard_map.126
  32.9 1.2 %shard_map.127 = (bf16[24,1024]{1,0:T(8,128)(2,1)S(1)}, bf16[24,1024]{1,0:T(8,128)(2,1)S(1)}, bf16[24,1024]{1,0:T(8,128)(2,1)S(1)}, bf16[24,1024]{1,0:T(8,128)(2,1)S(1)}) custom-call(f32[1,1024]{1,0:T(1,128)S(1)} %bitcast.27, bf16[1024,384]{1,0:T(8,128)(2,1)S(1)} %bitcast.17, bf16[1024,384]{1,0:T(8,128)(2,1)S(1)} %bitcast.19, ...), custom_call_target="tpu_custom_call" | custom-call | flops 2300000000 | bytes 5296128 | tf_op jit(solution)/shard_map/pallas_call | solution.py:271
  34.1 2.9 %collective-permute-start.10 = (bf16[24,1024]{1,0:T(8,128)(2,1)S(1)}, bf16[24,1024]{1,0:T(8,128)(2,1)S(1)}, u32[]{:S(2)}, u32[]{:S(2)}) collective-permute-start(bf16[24,1024]{1,0:T(8,128)(2,1)S(1)} %get-tuple-element.44), channel_id=1, source_target_pairs={{0,6},{2,4},{4,2},{6,0},{1,7},{3,5},{5,3},{7,1},{8,14},{10,12},{12... | collective-permute-start | bytes 147464 | tf_op jit(solution)/shard_map/ppermute | solution.py:287
  37.0 1.6 %collective-permute-start.12 = (bf16[24,1024]{1,0:T(8,128)(2,1)S(1)}, bf16[24,1024]{1,0:T(8,128)(2,1)S(1)}, u32[]{:S(2)}, u32[]{:S(2)}) collective-permute-start(bf16[24,1024]{1,0:T(8,128)(2,1)S(1)} %get-tuple-element.46), channel_id=1, source_target_pairs={{0,2},{2,0},{4,6},{6,4},{1,3},{3,1},{5,7},{7,5},{8,10},{10,8},{12,... | collective-permute-start | bytes 147464 | tf_op jit(solution)/shard_map/ppermute | solution.py:287
  38.6 1.0 %shard_map.124.hidden_ref = f32[192,1024]{1,0:T(8,128)S(1)} custom-call(bf16[192,2048]{1,0:T(8,128)(2,1)S(1)} %get-tuple-element.31.refs_1_.mark_ref.att_ref, bf16[192,1024]{1,0:T(8,128)(2,1)S(1)} %bitcast.23, bf16[512,1024]{1,0:T(8,128)(2,1)S(1)} %copy-done, bf16[512,1024]{1,0:T(8,128)(2,1)S(1)} %shard_map.123.refs_1_.refs_4_, ...), custom_call_target="tpu_custom_call" | custom-call | flops 2300000000 | bytes 6160384 | tf_op jit(solution)/shard_map/pallas_call | solution.py:271
  39.6 0.9 %collective-permute-done.10.refs_1_ = bf16[24,1024]{1,0:T(8,128)(2,1)S(1)} collective-permute-done((bf16[24,1024]{1,0:T(8,128)(2,1)S(1)}, bf16[24,1024]{1,0:T(8,128)(2,1)S(1)}, u32[]{:S(2)}, u32[]{:S(2)}) %collective-permute-start.10) | collective-permute-done | bytes 49184 | tf_op jit(solution)/shard_map/ppermute | solution.py:287
  40.5 1.6 %collective-permute-done.11.refs_2_ = bf16[24,1024]{1,0:T(8,128)(2,1)S(1)} collective-permute-done((bf16[24,1024]{1,0:T(8,128)(2,1)S(1)}, bf16[24,1024]{1,0:T(8,128)(2,1)S(1)}, u32[]{:S(2)}, u32[]{:S(2)}) %collective-permute-start.11) | collective-permute-done | bytes 49184 | tf_op jit(solution)/shard_map/ppermute | solution.py:287
  42.1 1.0 %shard_map.128 = bf16[192,1024]{1,0:T(8,128)(2,1)} custom-call(f32[192,1024]{1,0:T(8,128)S(1)} %shard_map.124.hidden_ref, bf16[192,192]{1,0:T(8,128)(2,1)S(1)} %get-tuple-element.34.mix_ref, bf16[24,1024]{1,0:T(8,128)(2,1)S(1)} %get-tuple-element.43.refs_0_, bf16[24,1024]{1,0:T(8,128)(2,1)S(1)} %collective-permute-done.10.refs_1_, ...), custom_call_target="tpu_custom_call" | custom-call | flops 1150000000 | bytes 1449984 | tf_op jit(solution)/shard_map/pallas_call | solution.py:271
  (34 shorter events, 0.2 us)
Async XLA Ops:
  1.0 4.6 %copy-start = (bf16[512,1024]{1,0:T(8,128)(2,1)S(1)}, bf16[512,1024]{1,0:T(8,128)(2,1)}, u32[]{:S(2)}) copy-start(bf16[512,1024]{1,0:T(8,128)(2,1)} %refs_0_.3) | copy-start | bytes 3145732
  1.0 4.6 %copy-start.1 = (bf16[1,192,2048]{2,1,0:T(8,128)(2,1)S(1)}, bf16[1,192,2048]{2,1,0:T(8,128)(2,1)}, u32[]{:S(2)}) copy-start(bf16[1,192,2048]{2,1,0:T(8,128)(2,1)} %param.12) | copy-start | bytes 2359300
  1.0 4.5 %copy-start.9 = (s32[1,768]{1,0:T(1,128)S(1)}, s32[1,768]{1,0:T(1,128)}, u32[]{:S(2)}) copy-start(s32[1,768]{1,0:T(1,128)} %segs_ref.3) | copy-start | bytes 9220
  1.0 13.0 %collective-permute-start.1 = (bf16[192,512]{1,0:T(8,128)(2,1)S(1)}, bf16[192,512]{1,0:T(8,128)(2,1)S(1)}, u32[]{:S(2)}, u32[]{:S(2)}) collective-permute-start(bf16[192,512]{1,0:T(8,128)(2,1)S(1)} %pad_maximum_fusion.refs_0_.kv_ref), channel_id=1, source_target_pairs={{0,16},{8,24},{16,0},{24,8},{1,17},{9,25},{17,1},{25,9},{2,18},{10... | collective-permute-start | bytes 589832 | tf_op jit(solution)/shard_map/ppermute | solution.py:386
  4.0 9.9 %collective-permute-start = (bf16[192,512]{1,0:T(8,128)(2,1)S(1)}, bf16[192,512]{1,0:T(8,128)(2,1)S(1)}, u32[]{:S(2)}, u32[]{:S(2)}) collective-permute-start(bf16[192,512]{1,0:T(8,128)(2,1)S(1)} %pad_maximum_fusion.refs_0_.kv_ref), channel_id=1, source_target_pairs={{0,8},{8,16},{16,24},{24,0},{1,9},{9,17},{17,25},{25,1},{2,10},{10... | collective-permute-start | bytes 589832 | tf_op jit(solution)/shard_map/ppermute | solution.py:386
  5.5 4.0 %copy-start.5 = (bf16[1,192,1024]{2,1,0:T(8,128)(2,1)S(1)}, bf16[1,192,1024]{2,1,0:T(8,128)(2,1)}, u32[]{:S(2)}) copy-start(bf16[1,192,1024]{2,1,0:T(8,128)(2,1)} %param.16) | copy-start | bytes 1179652
  5.5 4.0 %copy-start.6 = (s32[1,192,8]{1,2,0:T(8,128)S(1)}, s32[1,192,8]{1,2,0:T(8,128)}, u32[]{:S(2)}) copy-start(s32[1,192,8]{1,2,0:T(8,128)} %param.19) | copy-start | bytes 18436
  5.6 4.0 %copy-start.7 = (f32[1,192,8]{1,2,0:T(8,128)S(1)}, f32[1,192,8]{1,2,0:T(8,128)}, u32[]{:S(2)}) copy-start(f32[1,192,8]{1,2,0:T(8,128)} %param.20) | copy-start | bytes 18436
  7.4 9.3 %collective-permute-start.2 = (bf16[256,1024]{1,0:T(8,128)(2,1)S(1)}, bf16[256,1024]{1,0:T(8,128)(2,1)S(1)}, u32[]{:S(2)}, u32[]{:S(2)}) collective-permute-start(bf16[256,1024]{1,0:T(8,128)(2,1)S(1)} %get-tuple-element.32), channel_id=1, source_target_pairs={{0,8},{1,17},{8,0},{9,25},{16,24},{17,1},{24,16},{25,9},{2,10},{3,... | collective-permute-start | bytes 1572872 | tf_op jit(solution)/shard_map/ppermute | solution.py:315
  7.5 16.2 %collective-permute-start.3 = (bf16[256,1024]{1,0:T(8,128)(2,1)S(1)}, bf16[256,1024]{1,0:T(8,128)(2,1)S(1)}, u32[]{:S(2)}, u32[]{:S(2)}) collective-permute-start(bf16[256,1024]{1,0:T(8,128)(2,1)S(1)} %get-tuple-element.33), channel_id=1, source_target_pairs={{0,8},{1,17},{8,0},{9,25},{16,24},{17,1},{24,16},{25,9},{2,10},{3,... | collective-permute-start | bytes 1572872 | tf_op jit(solution)/shard_map/ppermute | solution.py:316
  9.5 4.4 %copy-start.2 = (bf16[1,1024,384]{2,1,0:T(8,128)(2,1)S(1)}, bf16[1,1024,384]{2,1,0:T(8,128)(2,1)}, u32[]{:S(2)}) copy-start(bf16[1,1024,384]{2,1,0:T(8,128)(2,1)} %param.21) | copy-start | bytes 2359300
  9.5 4.4 %copy-start.3 = (bf16[1,1024,384]{2,1,0:T(8,128)(2,1)S(1)}, bf16[1,1024,384]{2,1,0:T(8,128)(2,1)}, u32[]{:S(2)}) copy-start(bf16[1,1024,384]{2,1,0:T(8,128)(2,1)} %param.22) | copy-start | bytes 2359300
  9.6 4.4 %copy-start.4 = (bf16[1,384,1024]{2,1,0:T(8,128)(2,1)S(1)}, bf16[1,384,1024]{2,1,0:T(8,128)(2,1)}, u32[]{:S(2)}) copy-start(bf16[1,384,1024]{2,1,0:T(8,128)(2,1)} %param.23) | copy-start | bytes 2359300
  9.6 4.4 %copy-start.8 = (f32[1024]{0:T(1024)S(1)}, f32[1024]{0:T(1024)}, u32[]{:S(2)}) copy-start(f32[1024]{0:T(1024)} %param.18) | copy-start | bytes 12292
  16.8 13.2 %collective-permute-start.4 = (bf16[256,1024]{1,0:T(8,128)(2,1)S(1)}, bf16[256,1024]{1,0:T(8,128)(2,1)S(1)}, u32[]{:S(2)}, u32[]{:S(2)}) collective-permute-start(bf16[256,1024]{1,0:T(8,128)(2,1)S(1)} %shard_map.122.first_ref.refs_1_), channel_id=1, source_target_pairs={{0,16},{1,9},{8,24},{9,1},{16,0},{17,25},{24,8},{25,17},{2,18},{3,... | collective-permute-start | bytes 1572872 | tf_op jit(solution)/shard_map/ppermute | solution.py:318
  19.3 10.7 %collective-permute-start.7 = (bf16[24,2304]{1,0:T(8,128)(2,1)S(1)}, bf16[24,2304]{1,0:T(8,128)(2,1)S(1)}, u32[]{:S(2)}, u32[]{:S(2)}) collective-permute-start(bf16[24,2304]{1,0:T(8,128)(2,1)S(1)} %get-tuple-element.38), channel_id=1, source_target_pairs={{0,6},{2,4},{4,2},{6,0},{1,7},{3,5},{5,3},{7,1},{8,14},{10,12},{12... | collective-permute-start | bytes 331784 | tf_op jit(solution)/shard_map/ppermute | solution.py:287
  23.0 9.7 %collective-permute-start.8 = (bf16[24,2304]{1,0:T(8,128)(2,1)S(1)}, bf16[24,2304]{1,0:T(8,128)(2,1)S(1)}, u32[]{:S(2)}, u32[]{:S(2)}) collective-permute-start(bf16[24,2304]{1,0:T(8,128)(2,1)S(1)} %get-tuple-element.39), channel_id=1, source_target_pairs={{0,4},{2,6},{4,0},{6,2},{1,5},{3,7},{5,1},{7,3},{8,12},{10,14},{12... | collective-permute-start | bytes 331784 | tf_op jit(solution)/shard_map/ppermute | solution.py:287
  23.0 9.7 %collective-permute-start.9 = (bf16[24,2304]{1,0:T(8,128)(2,1)S(1)}, bf16[24,2304]{1,0:T(8,128)(2,1)S(1)}, u32[]{:S(2)}, u32[]{:S(2)}) collective-permute-start(bf16[24,2304]{1,0:T(8,128)(2,1)S(1)} %get-tuple-element.40), channel_id=1, source_target_pairs={{0,2},{2,0},{4,6},{6,4},{1,3},{3,1},{5,7},{7,5},{8,10},{10,8},{12,... | collective-permute-start | bytes 331784 | tf_op jit(solution)/shard_map/ppermute | solution.py:287
  23.8 9.1 %collective-permute-start.5 = (bf16[512,1024]{1,0:T(8,128)(2,1)S(1)}, bf16[512,1024]{1,0:T(8,128)(2,1)S(1)}, u32[]{:S(2)}, u32[]{:S(2)}) collective-permute-start(bf16[512,1024]{1,0:T(8,128)(2,1)S(1)} %shard_map.123.refs_1_.refs_4_), channel_id=1, source_target_pairs={{0,1},{1,0},{2,3},{3,2},{4,5},{5,4},{6,7},{7,6},{8,9},{9,8},{10,11... | collective-permute-start | bytes 3145736 | tf_op jit(solution)/shard_map/ppermute | solution.py:330
  30.0 2.9 %collective-permute-start.6 = (bf16[256,1024]{1,0:T(8,128)(2,1)S(1)}, bf16[256,1024]{1,0:T(8,128)(2,1)S(1)}, u32[]{:S(2)}, u32[]{:S(2)}) collective-permute-start(bf16[256,1024]{1,0:T(8,128)(2,1)S(1)} %collective-permute-done.4.refs_2_.refs_0_), channel_id=1, source_target_pairs={{0,1},{1,0},{2,3},{3,2},{4,5},{5,4},{6,7},{7,6},{8,9},{9,8},{10,11... | collective-permute-start | bytes 1572872 | tf_op jit(solution)/shard_map/ppermute | solution.py:330
  34.1 6.4 %collective-permute-start.10 = (bf16[24,1024]{1,0:T(8,128)(2,1)S(1)}, bf16[24,1024]{1,0:T(8,128)(2,1)S(1)}, u32[]{:S(2)}, u32[]{:S(2)}) collective-permute-start(bf16[24,1024]{1,0:T(8,128)(2,1)S(1)} %get-tuple-element.44), channel_id=1, source_target_pairs={{0,6},{2,4},{4,2},{6,0},{1,7},{3,5},{5,3},{7,1},{8,14},{10,12},{12... | collective-permute-start | bytes 147464 | tf_op jit(solution)/shard_map/ppermute | solution.py:287
  37.0 5.0 %collective-permute-start.11 = (bf16[24,1024]{1,0:T(8,128)(2,1)S(1)}, bf16[24,1024]{1,0:T(8,128)(2,1)S(1)}, u32[]{:S(2)}, u32[]{:S(2)}) collective-permute-start(bf16[24,1024]{1,0:T(8,128)(2,1)S(1)} %get-tuple-element.45), channel_id=1, source_target_pairs={{0,4},{2,6},{4,0},{6,2},{1,5},{3,7},{5,1},{7,3},{8,12},{10,14},{12... | collective-permute-start | bytes 147464 | tf_op jit(solution)/shard_map/ppermute | solution.py:287
  37.0 5.1 %collective-permute-start.12 = (bf16[24,1024]{1,0:T(8,128)(2,1)S(1)}, bf16[24,1024]{1,0:T(8,128)(2,1)S(1)}, u32[]{:S(2)}, u32[]{:S(2)}) collective-permute-start(bf16[24,1024]{1,0:T(8,128)(2,1)S(1)} %get-tuple-element.46), channel_id=1, source_target_pairs={{0,2},{2,0},{4,6},{6,4},{1,3},{3,1},{5,7},{7,5},{8,10},{10,8},{12,... | collective-permute-start | bytes 147464 | tf_op jit(solution)/shard_map/ppermute | solution.py:287
where the time goes:
time: 43.2 us; the launch traced here: 43.1 us
  starting transfers between devices  22.3 us (52%)
  waiting for transfers between devices  10.6 us (25%)
  Pallas kernels  8.97 us (21%)
  other arithmetic  0.95 us (2%)
    pallas_call x10, Pallas kernels, call(): pl.pallas_call(kernel, out_shape=outs, in_specs=[vmem] * (len(args) - fre...  8.97 us
    ppermute x6, starting transfers between devices, exchange(): lax.ppermute(blocks[s], 'exp', [(i, i ^ s) for i in range(count)])  8.9 us
    ppermute x6, waiting for transfers between devices, exchange(): lax.ppermute(blocks[s], 'exp', [(i, i ^ s) for i in range(count)])  5.16 us
    ppermute x1, starting transfers between devices, gather_weight(): lax.ppermute(near, 'dp', swap)  4.72 us
    ppermute x2, starting transfers between devices, per_device(): kv_blocks.append(lax.ppermute(own_kv, 'ctx', pairs))  4.52 us
    ppermute x2, waiting for transfers between devices, per_device(): kv_blocks.append(lax.ppermute(own_kv, 'ctx', pairs))  4 us
    ppermute x1, starting transfers between devices, gather_weight(): far = lax.ppermute(near_first, both, across)  2.04 us
    ppermute x1, starting transfers between devices, gather_weight(): near_second = lax.ppermute(second, both, aside)  1.99 us
  transfers between devices with their start and end apart: 13, of which 5 were waited for; matrix products, arithmetic and copies ran while one was open for 0% of the time, Pallas kernels for 16%

commit v1 on v0

--- a/solution.py
+++ b/solution.py
@@ -231,7 +231,7 @@
 
 def arrive_kernel(owners, entries, *refs):
     row_refs, piece_refs, (att_ref, hidden_ref) = refs[:owners], refs[owners:-2], refs[-2:]
-    row_refs = row_refs[:1] + row_refs[:0:-1]
+    row_refs = in_order(row_refs)
     wide = att_ref.shape[1]
     att_ref[...] = stack([ref[:, :wide] for ref in row_refs])
     hidden = jnp.concatenate([ref[:, wide:].astype(F32) for ref in row_refs], axis=0)
@@ -257,7 +257,7 @@
 
 
 def combine_kernel(owners, hidden_ref, mix_ref, *refs):
-    row_refs, out_ref = refs[:1] + refs[owners - 1 : 0 : -1], refs[owners]
+    row_refs, out_ref = in_order(refs[:owners]), refs[owners]
     rows = stack([ref[...] for ref in row_refs])
     total = hidden_ref[...] + jnp.dot(
         mix_ref[...], jnp.concatenate([rows, rows], axis=0), preferred_element_type=F32
@@ -281,11 +281,20 @@
     )(*args)
 
 
+def far_first(count):
+    return sorted(range(1, count), key=lambda s: (-s.bit_length(), s))
+
+
+def in_order(refs):
+    order = far_first(len(refs))
+    return [refs[0]] + [refs[1 + order.index(s)] for s in range(1, len(refs))]
+
+
 def exchange(blocks):
     count = len(blocks)
     return [blocks[0]] + [
         lax.ppermute(blocks[s], "exp", [(i, i ^ s) for i in range(count)])
-        for s in range(count - 1, 0, -1)
+        for s in far_first(count)
     ]
 
 

time: 43.2 us -> 43.7 us (1.012)
  waiting for transfers between devices: 10.6 us -> 11.1 us
  transfers between devices with their start and end apart: 13 -> 13, of which waited for: 5 -> 7; matrix products, arithmetic and copies ran while one was open for 0% -> 0% of each run, Pallas kernels for 16% -> 16%
where the time goes in v1:
time: 43.7 us; the launch traced here: 43.6 us
  starting transfers between devices  22.3 us (51%)
  waiting for transfers between devices  11.1 us (25%)
  Pallas kernels  8.97 us (21%)
  other arithmetic  0.95 us (2%)
    pallas_call x10, Pallas kernels, call(): pl.pallas_call(kernel, out_shape=outs, in_specs=[vmem] * (len(args) - fre...  8.96 us
    ppermute x6, starting transfers between devices, exchange(): lax.ppermute(blocks[s], 'exp', [(i, i ^ s) for i in range(count)])  8.76 us
    ppermute x6, waiting for transfers between devices, exchange(): lax.ppermute(blocks[s], 'exp', [(i, i ^ s) for i in range(count)])  5.51 us
    ppermute x1, starting transfers between devices, gather_weight(): lax.ppermute(near, 'dp', swap)  4.87 us
    ppermute x2, starting transfers between devices, per_device(): kv_blocks.append(lax.ppermute(own_kv, 'ctx', pairs))  4.52 us
    ppermute x2, waiting for transfers between devices, per_device(): kv_blocks.append(lax.ppermute(own_kv, 'ctx', pairs))  4 us
    ppermute x1, starting transfers between devices, gather_weight(): far = lax.ppermute(near_first, both, across)  2.04 us
    ppermute x1, starting transfers between devices, gather_weight(): near_second = lax.ppermute(second, both, aside)  1.99 us
  transfers between devices with their start and end apart: 13, of which 7 were waited for; matrix products, arithmetic and copies ran while one was open for 0% of the time, Pallas kernels for 16%

profile of v1, /device:TPU:0, one launch (start us, length us, event | category | flops | bytes accessed | tf_op | source)
XLA Modules:
  0.0 43.6 jit_solution(15241239036654139694)
XLA Ops:
  0.0 1.0 %pad_maximum_fusion.refs_0_.kv_ref = bf16[192,512]{1,0:T(8,128)(2,1)S(1)} fusion(bf16[192,256]{1,0:T(8,128)(2,1)} %bitcast.28, bf16[192,256]{1,0:T(8,128)(2,1)} %bitcast.29), kind=kLoop, calls=%fused_computation | loop fusion | flops 393216 | bytes 393216 | tf_op jit(solution)/shard_map/concatenate | solution.py:391
  1.0 3.0 %collective-permute-start.1 = (bf16[192,512]{1,0:T(8,128)(2,1)S(1)}, bf16[192,512]{1,0:T(8,128)(2,1)S(1)}, u32[]{:S(2)}, u32[]{:S(2)}) collective-permute-start(bf16[192,512]{1,0:T(8,128)(2,1)S(1)} %pad_maximum_fusion.refs_0_.kv_ref), channel_id=1, source_target_pairs={{0,16},{8,24},{16,0},{24,8},{1,17},{9,25},{17,1},{25,9},{2,18},{10... | collective-permute-start | bytes 589832 | tf_op jit(solution)/shard_map/ppermute | solution.py:395
  4.0 1.5 %collective-permute-start = (bf16[192,512]{1,0:T(8,128)(2,1)S(1)}, bf16[192,512]{1,0:T(8,128)(2,1)S(1)}, u32[]{:S(2)}, u32[]{:S(2)}) collective-permute-start(bf16[192,512]{1,0:T(8,128)(2,1)S(1)} %pad_maximum_fusion.refs_0_.kv_ref), channel_id=1, source_target_pairs={{0,8},{8,16},{16,24},{24,0},{1,9},{9,17},{17,25},{25,1},{2,10},{10... | collective-permute-start | bytes 589832 | tf_op jit(solution)/shard_map/ppermute | solution.py:395
  5.6 1.9 %shard_map.119 = (f32[2,8,192,128]{3,2,1,0:T(8,128)S(1)}, f32[2,8,192,128]{3,2,1,0:T(8,128)S(1)}, f32[2,8,192,128]{3,2,1,0:T(8,128)S(1)}, bf16[2,1536,128]{2,1,0...) custom-call(bf16[192,2048]{1,0:T(8,128)(2,1)S(1)} %bitcast.15, ...), custom_call_target="tpu_custom_call" | custom-call | flops 3449999872 | bytes 8592384 | tf_op jit(solution)/shard_map/pallas_call | solution.py:271
  7.5 2.0 %collective-permute-start.3 = (bf16[256,1024]{1,0:T(8,128)(2,1)S(1)}, bf16[256,1024]{1,0:T(8,128)(2,1)S(1)}, u32[]{:S(2)}, u32[]{:S(2)}) collective-permute-start(bf16[256,1024]{1,0:T(8,128)(2,1)S(1)} %get-tuple-element.33), channel_id=1, source_target_pairs={{0,8},{1,17},{8,0},{9,25},{16,24},{17,1},{24,16},{25,9},{2,10},{3,... | collective-permute-start | bytes 1572872 | tf_op jit(solution)/shard_map/ppermute | solution.py:325
  9.6 0.4 shard_map.120
  10.0 4.0 %collective-permute-done.1.refs_1_ = bf16[192,512]{1,0:T(8,128)(2,1)S(1)} collective-permute-done((bf16[192,512]{1,0:T(8,128)(2,1)S(1)}, bf16[192,512]{1,0:T(8,128)(2,1)S(1)}, u32[]{:S(2)}, u32[]{:S(2)}) %collective-permute-start.1) | collective-permute-done | bytes 196640 | tf_op jit(solution)/shard_map/ppermute | solution.py:395
  14.0 2.8 %shard_map.121 = (bf16[192,2048]{1,0:T(8,128)(2,1)S(1)}, f32[96,2048]{1,0:T(8,128)S(1)}) custom-call(s32[1,768]{1,0:T(1,128)S(1)} %copy-done.9, f32[2,8,192,128]{3,2,1,0:T(8,128)S(1)} %get-tuple-element.26.acc_ref, f32[2,8,192,128]{3,2,1,0:T(8,128)S(1)} %get-tuple-element.27.max_ref, f32[2,8,192,128]{3,2,1,0:T(8,128)S(1)} %get-tuple-element.28.sum_ref, ...), custom_call_target="tpu_custom_call" | custom-call | flops 5750000128 | bytes 9874432 | tf_op jit(solution)/shard_map/pallas_call | solution.py:271
  16.8 2.0 %collective-permute-start.4 = (bf16[256,1024]{1,0:T(8,128)(2,1)S(1)}, bf16[256,1024]{1,0:T(8,128)(2,1)S(1)}, u32[]{:S(2)}, u32[]{:S(2)}) collective-permute-start(bf16[256,1024]{1,0:T(8,128)(2,1)S(1)} %shard_map.122.first_ref.refs_1_), channel_id=1, source_target_pairs={{0,16},{1,9},{8,24},{9,1},{16,0},{17,25},{24,8},{25,17},{2,18},{3,... | collective-permute-start | bytes 1572872 | tf_op jit(solution)/shard_map/ppermute | solution.py:327
  18.9 0.4 shard_map.125
  19.3 2.7 %collective-permute-start.7 = (bf16[24,2304]{1,0:T(8,128)(2,1)S(1)}, bf16[24,2304]{1,0:T(8,128)(2,1)S(1)}, u32[]{:S(2)}, u32[]{:S(2)}) collective-permute-start(bf16[24,2304]{1,0:T(8,128)(2,1)S(1)} %get-tuple-element.38), channel_id=1, source_target_pairs={{0,4},{2,6},{4,0},{6,2},{1,5},{3,7},{5,1},{7,3},{8,12},{10,14},{12... | collective-permute-start | bytes 331784 | tf_op jit(solution)/shard_map/ppermute | solution.py:296
  22.0 1.3 %collective-permute-start.8 = (bf16[24,2304]{1,0:T(8,128)(2,1)S(1)}, bf16[24,2304]{1,0:T(8,128)(2,1)S(1)}, u32[]{:S(2)}, u32[]{:S(2)}) collective-permute-start(bf16[24,2304]{1,0:T(8,128)(2,1)S(1)} %get-tuple-element.39), channel_id=1, source_target_pairs={{0,6},{2,4},{4,2},{6,0},{1,7},{3,5},{5,3},{7,1},{8,14},{10,12},{12... | collective-permute-start | bytes 331784 | tf_op jit(solution)/shard_map/ppermute | solution.py:296
  23.7 4.9 %collective-permute-start.5 = (bf16[512,1024]{1,0:T(8,128)(2,1)S(1)}, bf16[512,1024]{1,0:T(8,128)(2,1)S(1)}, u32[]{:S(2)}, u32[]{:S(2)}) collective-permute-start(bf16[512,1024]{1,0:T(8,128)(2,1)S(1)} %shard_map.123.refs_1_.refs_4_), channel_id=1, source_target_pairs={{0,1},{1,0},{2,3},{3,2},{4,5},{5,4},{6,7},{7,6},{8,9},{9,8},{10,11... | collective-permute-start | bytes 3145736 | tf_op jit(solution)/shard_map/ppermute | solution.py:339
  28.5 1.5 %collective-permute-done.4.refs_2_.refs_0_ = bf16[256,1024]{1,0:T(8,128)(2,1)S(1)} collective-permute-done((bf16[256,1024]{1,0:T(8,128)(2,1)S(1)}, bf16[256,1024]{1,0:T(8,128)(2,1)S(1)}, u32[]{:S(2)}, u32[]{:S(2)}) %collective-permute-start.4) | collective-permute-done | bytes 524320 | tf_op jit(solution)/shard_map/ppermute | solution.py:327
  30.0 0.9 %collective-permute-done.7.refs_1_ = bf16[24,2304]{1,0:T(8,128)(2,1)S(1)} collective-permute-done((bf16[24,2304]{1,0:T(8,128)(2,1)S(1)}, bf16[24,2304]{1,0:T(8,128)(2,1)S(1)}, u32[]{:S(2)}, u32[]{:S(2)}) %collective-permute-start.7) | collective-permute-done | bytes 110624 | tf_op jit(solution)/shard_map/ppermute | solution.py:296
  30.9 0.6 %collective-permute-done.9.refs_3_ = bf16[24,2304]{1,0:T(8,128)(2,1)S(1)} collective-permute-done((bf16[24,2304]{1,0:T(8,128)(2,1)S(1)}, bf16[24,2304]{1,0:T(8,128)(2,1)S(1)}, u32[]{:S(2)}, u32[]{:S(2)}) %collective-permute-start.9) | collective-permute-done | bytes 110624 | tf_op jit(solution)/shard_map/ppermute | solution.py:296
  31.5 0.2 shard_map.126
  31.9 1.2 %shard_map.127 = (bf16[24,1024]{1,0:T(8,128)(2,1)S(1)}, bf16[24,1024]{1,0:T(8,128)(2,1)S(1)}, bf16[24,1024]{1,0:T(8,128)(2,1)S(1)}, bf16[24,1024]{1,0:T(8,128)(2,1)S(1)}) custom-call(f32[1,1024]{1,0:T(1,128)S(1)} %bitcast.27, bf16[1024,384]{1,0:T(8,128)(2,1)S(1)} %bitcast.17, bf16[1024,384]{1,0:T(8,128)(2,1)S(1)} %bitcast.19, ...), custom_call_target="tpu_custom_call" | custom-call | flops 2300000000 | bytes 5296128 | tf_op jit(solution)/shard_map/pallas_call | solution.py:271
  33.1 3.6 %collective-permute-start.10 = (bf16[24,1024]{1,0:T(8,128)(2,1)S(1)}, bf16[24,1024]{1,0:T(8,128)(2,1)S(1)}, u32[]{:S(2)}, u32[]{:S(2)}) collective-permute-start(bf16[24,1024]{1,0:T(8,128)(2,1)S(1)} %get-tuple-element.44), channel_id=1, source_target_pairs={{0,4},{2,6},{4,0},{6,2},{1,5},{3,7},{5,1},{7,3},{8,12},{10,14},{12... | collective-permute-start | bytes 147464 | tf_op jit(solution)/shard_map/ppermute | solution.py:296
  36.7 0.6 %collective-permute-start.11 = (bf16[24,1024]{1,0:T(8,128)(2,1)S(1)}, bf16[24,1024]{1,0:T(8,128)(2,1)S(1)}, u32[]{:S(2)}, u32[]{:S(2)}) collective-permute-start(bf16[24,1024]{1,0:T(8,128)(2,1)S(1)} %get-tuple-element.45), channel_id=1, source_target_pairs={{0,6},{2,4},{4,2},{6,0},{1,7},{3,5},{5,3},{7,1},{8,14},{10,12},{12... | collective-permute-start | bytes 147464 | tf_op jit(solution)/shard_map/ppermute | solution.py:296
  37.6 1.0 %shard_map.124.hidden_ref = f32[192,1024]{1,0:T(8,128)S(1)} custom-call(bf16[192,2048]{1,0:T(8,128)(2,1)S(1)} %get-tuple-element.31.refs_1_.mark_ref.att_ref, bf16[192,1024]{1,0:T(8,128)(2,1)S(1)} %bitcast.23, bf16[512,1024]{1,0:T(8,128)(2,1)S(1)} %copy-done, bf16[512,1024]{1,0:T(8,128)(2,1)S(1)} %shard_map.123.refs_1_.refs_4_, ...), custom_call_target="tpu_custom_call" | custom-call | flops 2300000000 | bytes 6160384 | tf_op jit(solution)/shard_map/pallas_call | solution.py:271
  38.6 1.4 %collective-permute-done.10.refs_1_ = bf16[24,1024]{1,0:T(8,128)(2,1)S(1)} collective-permute-done((bf16[24,1024]{1,0:T(8,128)(2,1)S(1)}, bf16[24,1024]{1,0:T(8,128)(2,1)S(1)}, u32[]{:S(2)}, u32[]{:S(2)}) %collective-permute-start.10) | collective-permute-done | bytes 49184 | tf_op jit(solution)/shard_map/ppermute | solution.py:296
  39.9 2.6 %collective-permute-done.11.refs_2_ = bf16[24,1024]{1,0:T(8,128)(2,1)S(1)} collective-permute-done((bf16[24,1024]{1,0:T(8,128)(2,1)S(1)}, bf16[24,1024]{1,0:T(8,128)(2,1)S(1)}, u32[]{:S(2)}, u32[]{:S(2)}) %collective-permute-start.11) | collective-permute-done | bytes 49184 | tf_op jit(solution)/shard_map/ppermute | solution.py:296
  42.6 1.0 %shard_map.128 = bf16[192,1024]{1,0:T(8,128)(2,1)} custom-call(f32[192,1024]{1,0:T(8,128)S(1)} %shard_map.124.hidden_ref, bf16[192,192]{1,0:T(8,128)(2,1)S(1)} %get-tuple-element.34.mix_ref, bf16[24,1024]{1,0:T(8,128)(2,1)S(1)} %get-tuple-element.43.refs_0_, bf16[24,1024]{1,0:T(8,128)(2,1)S(1)} %collective-permute-done.10.refs_1_, ...), custom_call_target="tpu_custom_call" | custom-call | flops 1150000000 | bytes 1449984 | tf_op jit(solution)/shard_map/pallas_call | solution.py:271
  (34 shorter events, 0.9 us)
Async XLA Ops:
  1.0 4.6 %copy-start = (bf16[512,1024]{1,0:T(8,128)(2,1)S(1)}, bf16[512,1024]{1,0:T(8,128)(2,1)}, u32[]{:S(2)}) copy-start(bf16[512,1024]{1,0:T(8,128)(2,1)} %refs_0_.3) | copy-start | bytes 3145732
  1.0 4.6 %copy-start.1 = (bf16[1,192,2048]{2,1,0:T(8,128)(2,1)S(1)}, bf16[1,192,2048]{2,1,0:T(8,128)(2,1)}, u32[]{:S(2)}) copy-start(bf16[1,192,2048]{2,1,0:T(8,128)(2,1)} %param.12) | copy-start | bytes 2359300
  1.0 4.5 %copy-start.9 = (s32[1,768]{1,0:T(1,128)S(1)}, s32[1,768]{1,0:T(1,128)}, u32[]{:S(2)}) copy-start(s32[1,768]{1,0:T(1,128)} %segs_ref.3) | copy-start | bytes 9220
  1.0 13.0 %collective-permute-start.1 = (bf16[192,512]{1,0:T(8,128)(2,1)S(1)}, bf16[192,512]{1,0:T(8,128)(2,1)S(1)}, u32[]{:S(2)}, u32[]{:S(2)}) collective-permute-start(bf16[192,512]{1,0:T(8,128)(2,1)S(1)} %pad_maximum_fusion.refs_0_.kv_ref), channel_id=1, source_target_pairs={{0,16},{8,24},{16,0},{24,8},{1,17},{9,25},{17,1},{25,9},{2,18},{10... | collective-permute-start | bytes 589832 | tf_op jit(solution)/shard_map/ppermute | solution.py:395
  4.0 9.9 %collective-permute-start = (bf16[192,512]{1,0:T(8,128)(2,1)S(1)}, bf16[192,512]{1,0:T(8,128)(2,1)S(1)}, u32[]{:S(2)}, u32[]{:S(2)}) collective-permute-start(bf16[192,512]{1,0:T(8,128)(2,1)S(1)} %pad_maximum_fusion.refs_0_.kv_ref), channel_id=1, source_target_pairs={{0,8},{8,16},{16,24},{24,0},{1,9},{9,17},{17,25},{25,1},{2,10},{10... | collective-permute-start | bytes 589832 | tf_op jit(solution)/shard_map/ppermute | solution.py:395
  5.5 4.0 %copy-start.5 = (bf16[1,192,1024]{2,1,0:T(8,128)(2,1)S(1)}, bf16[1,192,1024]{2,1,0:T(8,128)(2,1)}, u32[]{:S(2)}) copy-start(bf16[1,192,1024]{2,1,0:T(8,128)(2,1)} %param.16) | copy-start | bytes 1179652
  5.5 4.0 %copy-start.6 = (s32[1,192,8]{1,2,0:T(8,128)S(1)}, s32[1,192,8]{1,2,0:T(8,128)}, u32[]{:S(2)}) copy-start(s32[1,192,8]{1,2,0:T(8,128)} %param.19) | copy-start | bytes 18436
  5.6 4.0 %copy-start.7 = (f32[1,192,8]{1,2,0:T(8,128)S(1)}, f32[1,192,8]{1,2,0:T(8,128)}, u32[]{:S(2)}) copy-start(f32[1,192,8]{1,2,0:T(8,128)} %param.20) | copy-start | bytes 18436
  7.4 9.3 %collective-permute-start.2 = (bf16[256,1024]{1,0:T(8,128)(2,1)S(1)}, bf16[256,1024]{1,0:T(8,128)(2,1)S(1)}, u32[]{:S(2)}, u32[]{:S(2)}) collective-permute-start(bf16[256,1024]{1,0:T(8,128)(2,1)S(1)} %get-tuple-element.32), channel_id=1, source_target_pairs={{0,8},{1,17},{8,0},{9,25},{16,24},{17,1},{24,16},{25,9},{2,10},{3,... | collective-permute-start | bytes 1572872 | tf_op jit(solution)/shard_map/ppermute | solution.py:324
  7.5 16.0 %collective-permute-start.3 = (bf16[256,1024]{1,0:T(8,128)(2,1)S(1)}, bf16[256,1024]{1,0:T(8,128)(2,1)S(1)}, u32[]{:S(2)}, u32[]{:S(2)}) collective-permute-start(bf16[256,1024]{1,0:T(8,128)(2,1)S(1)} %get-tuple-element.33), channel_id=1, source_target_pairs={{0,8},{1,17},{8,0},{9,25},{16,24},{17,1},{24,16},{25,9},{2,10},{3,... | collective-permute-start | bytes 1572872 | tf_op jit(solution)/shard_map/ppermute | solution.py:325
  9.5 4.4 %copy-start.2 = (bf16[1,1024,384]{2,1,0:T(8,128)(2,1)S(1)}, bf16[1,1024,384]{2,1,0:T(8,128)(2,1)}, u32[]{:S(2)}) copy-start(bf16[1,1024,384]{2,1,0:T(8,128)(2,1)} %param.21) | copy-start | bytes 2359300
  9.5 4.4 %copy-start.3 = (bf16[1,1024,384]{2,1,0:T(8,128)(2,1)S(1)}, bf16[1,1024,384]{2,1,0:T(8,128)(2,1)}, u32[]{:S(2)}) copy-start(bf16[1,1024,384]{2,1,0:T(8,128)(2,1)} %param.22) | copy-start | bytes 2359300
  9.6 4.4 %copy-start.4 = (bf16[1,384,1024]{2,1,0:T(8,128)(2,1)S(1)}, bf16[1,384,1024]{2,1,0:T(8,128)(2,1)}, u32[]{:S(2)}) copy-start(bf16[1,384,1024]{2,1,0:T(8,128)(2,1)} %param.23) | copy-start | bytes 2359300
  9.6 4.4 %copy-start.8 = (f32[1024]{0:T(1024)S(1)}, f32[1024]{0:T(1024)}, u32[]{:S(2)}) copy-start(f32[1024]{0:T(1024)} %param.18) | copy-start | bytes 12292
  16.8 13.2 %collective-permute-start.4 = (bf16[256,1024]{1,0:T(8,128)(2,1)S(1)}, bf16[256,1024]{1,0:T(8,128)(2,1)S(1)}, u32[]{:S(2)}, u32[]{:S(2)}) collective-permute-start(bf16[256,1024]{1,0:T(8,128)(2,1)S(1)} %shard_map.122.first_ref.refs_1_), channel_id=1, source_target_pairs={{0,16},{1,9},{8,24},{9,1},{16,0},{17,25},{24,8},{25,17},{2,18},{3,... | collective-permute-start | bytes 1572872 | tf_op jit(solution)/shard_map/ppermute | solution.py:327
  19.3 11.6 %collective-permute-start.7 = (bf16[24,2304]{1,0:T(8,128)(2,1)S(1)}, bf16[24,2304]{1,0:T(8,128)(2,1)S(1)}, u32[]{:S(2)}, u32[]{:S(2)}) collective-permute-start(bf16[24,2304]{1,0:T(8,128)(2,1)S(1)} %get-tuple-element.38), channel_id=1, source_target_pairs={{0,4},{2,6},{4,0},{6,2},{1,5},{3,7},{5,1},{7,3},{8,12},{10,14},{12... | collective-permute-start | bytes 331784 | tf_op jit(solution)/shard_map/ppermute | solution.py:296
  22.0 8.9 %collective-permute-start.8 = (bf16[24,2304]{1,0:T(8,128)(2,1)S(1)}, bf16[24,2304]{1,0:T(8,128)(2,1)S(1)}, u32[]{:S(2)}, u32[]{:S(2)}) collective-permute-start(bf16[24,2304]{1,0:T(8,128)(2,1)S(1)} %get-tuple-element.39), channel_id=1, source_target_pairs={{0,6},{2,4},{4,2},{6,0},{1,7},{3,5},{5,3},{7,1},{8,14},{10,12},{12... | collective-permute-start | bytes 331784 | tf_op jit(solution)/shard_map/ppermute | solution.py:296
  23.3 8.2 %collective-permute-start.9 = (bf16[24,2304]{1,0:T(8,128)(2,1)S(1)}, bf16[24,2304]{1,0:T(8,128)(2,1)S(1)}, u32[]{:S(2)}, u32[]{:S(2)}) collective-permute-start(bf16[24,2304]{1,0:T(8,128)(2,1)S(1)} %get-tuple-element.40), channel_id=1, source_target_pairs={{0,2},{2,0},{4,6},{6,4},{1,3},{3,1},{5,7},{7,5},{8,10},{10,8},{12,... | collective-permute-start | bytes 331784 | tf_op jit(solution)/shard_map/ppermute | solution.py:296
  23.7 8.2 %collective-permute-start.5 = (bf16[512,1024]{1,0:T(8,128)(2,1)S(1)}, bf16[512,1024]{1,0:T(8,128)(2,1)S(1)}, u32[]{:S(2)}, u32[]{:S(2)}) collective-permute-start(bf16[512,1024]{1,0:T(8,128)(2,1)S(1)} %shard_map.123.refs_1_.refs_4_), channel_id=1, source_target_pairs={{0,1},{1,0},{2,3},{3,2},{4,5},{5,4},{6,7},{7,6},{8,9},{9,8},{10,11... | collective-permute-start | bytes 3145736 | tf_op jit(solution)/shard_map/ppermute | solution.py:339
  30.0 1.9 %collective-permute-start.6 = (bf16[256,1024]{1,0:T(8,128)(2,1)S(1)}, bf16[256,1024]{1,0:T(8,128)(2,1)S(1)}, u32[]{:S(2)}, u32[]{:S(2)}) collective-permute-start(bf16[256,1024]{1,0:T(8,128)(2,1)S(1)} %collective-permute-done.4.refs_2_.refs_0_), channel_id=1, source_target_pairs={{0,1},{1,0},{2,3},{3,2},{4,5},{5,4},{6,7},{7,6},{8,9},{9,8},{10,11... | collective-permute-start | bytes 1572872 | tf_op jit(solution)/shard_map/ppermute | solution.py:339
  33.1 6.8 %collective-permute-start.10 = (bf16[24,1024]{1,0:T(8,128)(2,1)S(1)}, bf16[24,1024]{1,0:T(8,128)(2,1)S(1)}, u32[]{:S(2)}, u32[]{:S(2)}) collective-permute-start(bf16[24,1024]{1,0:T(8,128)(2,1)S(1)} %get-tuple-element.44), channel_id=1, source_target_pairs={{0,4},{2,6},{4,0},{6,2},{1,5},{3,7},{5,1},{7,3},{8,12},{10,14},{12... | collective-permute-start | bytes 147464 | tf_op jit(solution)/shard_map/ppermute | solution.py:296
  36.7 5.9 %collective-permute-start.11 = (bf16[24,1024]{1,0:T(8,128)(2,1)S(1)}, bf16[24,1024]{1,0:T(8,128)(2,1)S(1)}, u32[]{:S(2)}, u32[]{:S(2)}) collective-permute-start(bf16[24,1024]{1,0:T(8,128)(2,1)S(1)} %get-tuple-element.45), channel_id=1, source_target_pairs={{0,6},{2,4},{4,2},{6,0},{1,7},{3,5},{5,3},{7,1},{8,14},{10,12},{12... | collective-permute-start | bytes 147464 | tf_op jit(solution)/shard_map/ppermute | solution.py:296
  37.3 5.2 %collective-permute-start.12 = (bf16[24,1024]{1,0:T(8,128)(2,1)S(1)}, bf16[24,1024]{1,0:T(8,128)(2,1)S(1)}, u32[]{:S(2)}, u32[]{:S(2)}) collective-permute-start(bf16[24,1024]{1,0:T(8,128)(2,1)S(1)} %get-tuple-element.46), channel_id=1, source_target_pairs={{0,2},{2,0},{4,6},{6,4},{1,3},{3,1},{5,7},{7,5},{8,10},{10,8},{12,... | collective-permute-start | bytes 147464 | tf_op jit(solution)/shard_map/ppermute | solution.py:296
